TPU v7x, 256 devices: a whole 4x4x8 slice. The times are simulated.
256 devices in a mesh: slab: 8 (over x_hi, y), cell: 32 (over z, x_lo, core).
Axes of the slice: x: 4 (x_hi: 2, x_lo: 2; x = x_hi * 2 + x_lo), y: 4, z: 8, core: 2. Of those that a mesh axis runs over, the one named last changes fastest.
Arguments:
- positions: float32 [3, 2097152], P(None, ('slab', 'cell')), may hold values from 0 to 32, as said below
- burgers: float32 [3, 2097152], P(None, ('slab', 'cell')), may hold values from -0.018 to 0.018
- mobility: float32 [2097152], P(('slab', 'cell')), may hold values from 0.5 to 2
- near_list: int32 [16384, 6], P(('slab', 'cell')), may hold values from 0 to 255
- near_count: int32 [16384], P(('slab', 'cell')), may hold values from 1 to 6, as said below
- send_list: int32 [4, 12288], P(None, ('slab', 'cell')), may hold values from 0 to 63
Outputs:
- displacement: float32 [3, 2097152], P(None, ('slab', 'cell'))
- velocity: float32 [3, 2097152], P(None, ('slab', 'cell'))
Inputs may be any that keep to these rules, and one draw needn't show every extreme that they name: `positions`: cell (s, c) owns the segments of its block of 8192; every coordinate lies in that cell's box. `near_count`: some cells carry pile-ups with up to 6 live slots a block; the others have 1 or 2.
All inputs are finite; a program needn't handle non-finite values.
Results may differ from a plain program's by a relative error of at most 0.00035.
Values sent between devices are 32-bit elements; how exact they have to be, the bound alone decides.
No kernel may reach another device: no remote copies, remote signals or barrier semaphores. Data moves between devices by JAX's collectives and lax.ppermute only.
A program may use at most 128 MiB of HBM per device.

v0:
```python
import functools

import jax
import jax.numpy as jnp
from jax import lax
from jax.experimental import pallas as pl
from jax.experimental.pallas import tpu as pltpu
from jax.sharding import PartitionSpec as P

SUBSTEPS = 4
BLOCKS = 64
LANES = 128
NEAR = 6
GHOST = 48
EXT = 256
GROUP = 8
LEAD = GROUP
TAIL = 56
AT_SENDS = 8
AT_PAIRS = AT_SENDS + 4 * GHOST + LEAD
CONTROL = AT_PAIRS + BLOCKS * NEAR + TAIL + 8
SHARE = 9

core_sq = 0.04
far_sq = 1.0
time_step = 0.2

f32 = jnp.float32
bf16 = jnp.bfloat16

vmem = pl.BlockSpec(memory_space=pltpu.VMEM)
smem = pl.BlockSpec(memory_space=pltpu.SMEM)
params = pltpu.CompilerParams(vmem_limit_bytes=48 * 2**20)


def round_bf16(x):
    return x.astype(bf16).astype(f32)


def split2(x):
    high = x.astype(bf16)
    return high, (x - high.astype(f32)).astype(bf16)


def split3(x):
    high = round_bf16(x)
    rest = x - high
    mid = round_bf16(rest)
    return high, mid, round_bf16(rest - mid)


def parity():
    return lax.axis_index("slab") % 2, lax.axis_index("cell") % 2


def send_rows():
    odd_slab, odd_cell = parity()
    return odd_slab, 1 - odd_slab, 3 - odd_cell, 2 + odd_cell


def slot_moves():
    odd_slab, odd_cell = parity()
    return (
        GHOST * (1 - odd_slab),
        GHOST * (odd_slab - 1),
        GHOST * odd_cell,
        -GHOST * odd_cell,
    )


def slot_shifts():
    odd_slab, odd_cell = parity()
    along_slab = (1 - 2 * odd_slab).astype(f32)
    along_cell = (1 - 2 * odd_cell).astype(f32)
    return (0, along_slab), (0, -along_slab), (1, -along_cell), (1, along_cell)


def slot_exists():
    out = []
    for axis in ("slab", "cell"):
        i = lax.axis_index(axis)
        partner = i - 1 + 2 * (i % 2)
        out.append((partner >= 0) & (partner < lax.axis_size(axis)))
    return None, out[0], out[1], None


def fill_sends(block_of, sources, sends):
    def body(n, carry):
        for d in sends:
            block = block_of(d, n)
            for a, (ref, index) in enumerate(sources):
                sends[d][a, pl.ds(n, 1), :] = ref[index, pl.ds(block, 1), :]
        return carry

    lax.fori_loop(0, GHOST, body, 0, unroll=4)


def send_now(control, now, sends):
    fill_sends(
        lambda d, n: control[AT_SENDS + GHOST * d + n],
        [(now, k) for k in range(3)],
        dict(enumerate(sends)),
    )


def centre_of():
    slab = lax.axis_index("slab").astype(f32)
    cell = lax.axis_index("cell").astype(f32)
    return slab, cell


def list_pairs(near_list, near_count):
    segment = (near_list + (GHOST - BLOCKS)) // GHOST
    exists = {0: None, 3: None}
    exists[1], exists[2] = slot_exists()[1:3]
    odd_slab, odd_cell = parity()
    sides = (
        (odd_slab == 1) | exists[1],
        (odd_slab == 0) | exists[1],
        (odd_cell == 1) | exists[2],
        (odd_cell == 0) | exists[2],
    )
    slot = lax.broadcasted_iota(jnp.int32, near_list.shape, 0)
    block = lax.broadcasted_iota(jnp.int32, near_list.shape, 1)
    live = jnp.where(slot < near_count, 1, 0)
    moved = near_list
    for i, (move, there) in enumerate(zip(slot_moves(), sides)):
        mine = segment == 1 + i
        moved = moved + jnp.where(mine, move, 0)
        live = jnp.where(mine, live * there.astype(jnp.int32), live)
    rows = [live[i : i + 1] for i in range(NEAR)]
    before = [jnp.zeros_like(rows[0])]
    for row in rows:
        before.append(before[-1] + row)
    amount = before.pop().astype(f32)
    earlier = lax.broadcasted_iota(jnp.int32, (BLOCKS, BLOCKS), 0) < lax.broadcasted_iota(
        jnp.int32, (BLOCKS, BLOCKS), 1
    )
    offset = jnp.dot(
        jnp.broadcast_to(amount, (8, BLOCKS)), jnp.where(earlier, 1.0, 0.0), preferred_element_type=f32
    )[:1]
    at = jnp.concatenate([offset.astype(jnp.int32) + x for x in before], axis=0)
    at = jnp.where(live > 0, at, BLOCKS * NEAR + TAIL)
    words = 2**15 * at + 2**SHARE * block + moved
    return words, jnp.sum(amount, axis=1, keepdims=True).astype(jnp.int32)


def pack_kernel(numbers_smem, numbers, positions, burgers, places, scalars, s3, s0, s2, s1):
    slab, cell = centre_of()
    for k, by in enumerate((slab + 0.5, cell + 0.5, 0.5)):
        places[k] = positions[k] - by
    scalars[...] = jnp.zeros_like(scalars)
    words, amount = list_pairs(numbers[:NEAR, :BLOCKS], numbers[NEAR : NEAR + 1, :BLOCKS])
    scalars[:NEAR, :BLOCKS] = words
    scalars[NEAR : NEAR + 1, :] = jnp.broadcast_to(amount, (1, LANES))
    rows = send_rows()
    for d in range(4):
        first = 2 * (d // 2)
        scalars[8 + d : 9 + d, :] = jnp.where(
            rows[d] == first, numbers[8 + first : 9 + first, :], numbers[9 + first : 10 + first, :]
        )
    sources = [(places, k) for k in range(3)] + [(burgers, a) for a in range(3)]
    fill_sends(lambda d, n: numbers_smem[8 + rows[d], n], sources, {0: s0, 1: s1, 2: s2, 3: s3})


def put_rows(out, k, value):
    for b in range(BLOCKS):
        out[k : k + 1, LANES * b : LANES * b + LANES] = value[b : b + 1]


def halves(tile):
    low = lax.broadcasted_iota(jnp.int32, (8, LANES), 0) < 4
    turned = pltpu.roll(tile, 4, 0)
    return jnp.where(low, tile, turned), jnp.where(low, turned, tile)


def pair_rows(values):
    low = lax.broadcasted_iota(jnp.int32, (8, LANES), 0) < 4
    rows = [
        x if x is y else jnp.where(low, x, y) for x, y in zip(values[0::2], values[1::2])
    ]
    rows += [jnp.zeros((8, LANES), f32)] * (LANES // 8 - len(rows))
    return jnp.concatenate(rows, axis=0)


def far_kernel(
    scalars, places, burgers, out, control, acc, rows, cols, apart_by, w_even, w_odd
):
    amount = scalars[NEAR, 0]
    for i in range(LEAD):
        control[AT_PAIRS - LEAD + i] = EXT
    for tile in range(BLOCKS // 8):
        p = [halves(places[k, 8 * tile : 8 * tile + 8, :]) for k in range(3)]
        burg = [halves(burgers[a, 8 * tile : 8 * tile + 8, :]) for a in range(3)]
        for half in range(2):
            here = [x[half] for x in p]
            sources = [x[half] for x in burg]
            moments = [x * y for x in here for y in sources]
            values = []
            for group in (sources, moments):
                high = [round_bf16(x) for x in group]
                values += high + [x - h for x, h in zip(group, high)]
            rows[2 * tile + half] = pair_rows(values)
            one = jnp.ones((8, LANES), f32)
            square = sum(x * x for x in here) + far_sq
            values = [part for x in (here[0], here[1], square) for part in split3(x)]
            cols[2 * tile + half] = pair_rows(values + [one, one, one]).T.astype(bf16)
    acc[...] = jnp.zeros_like(acc)
    w_odd[...] = jnp.zeros_like(w_odd)
    slab, cell = centre_of()
    target = lax.broadcasted_iota(jnp.int32, (1, EXT), 1)
    apart = [(target // 32).astype(f32) - slab, (target % 32).astype(f32) - cell]
    square = apart[0] * apart[0] + apart[1] * apart[1]
    square_high = round_bf16(square)
    place = lax.broadcasted_iota(jnp.int32, (LANES, EXT), 0)
    values = jnp.where(place < 36, 1.0, 0.0)
    for first, last, x in (
        (0, 12, -2.0 * apart[0]),
        (12, 24, -2.0 * apart[1]),
        (36, 40, square_high),
        (40, 44, square - square_high),
    ):
        values = jnp.where((place >= first) & (place < last), x, values)
    for g in range(4):
        apart_by[g] = jnp.where(place % 4 == g, values, 0.0).astype(bf16)

    def sums(group, g, w):
        mine = rows[group, pl.ds(g, 32, stride=4), :].astype(bf16)
        acc[...] += jnp.dot(
            jnp.concatenate([mine, mine], axis=1), w[g], preferred_element_type=f32
        )

    def half(group, w_now, w_before):
        for i in range(4):
            for slot in range(NEAR):
                word = scalars[slot, 4 * group + i]
                at = lax.shift_right_logical(word, 15)
                control[AT_PAIRS + at] = word & (2**15 - 1)
        for d in range(4):
            for i in range(3):
                n = 3 * group + i
                control[AT_SENDS + GHOST * d + n] = scalars[8 + d, n]
        for g in range(4):
            sums(jnp.maximum(group - 1, 0), g, w_before)
            r = lax.rsqrt(jnp.dot(cols[group], apart_by[g], preferred_element_type=f32))
            r2 = r * r
            w3 = r2 * r
            for k, w in enumerate((w3, w3 * r2)):
                high, low = split2(w)
                w_now[g, :LANES, EXT * k : EXT * k + EXT] = high
                w_now[g, LANES:, EXT * k : EXT * k + EXT] = low

    def body(step, carry):
        half(2 * step, w_even, w_odd)
        half(2 * step + 1, w_odd, w_even)
        return carry

    lax.fori_loop(0, BLOCKS // 8, body, 0)
    for g in range(4):
        sums(BLOCKS // 4 - 1, g, w_odd)
    for i in range(TAIL):
        control[AT_PAIRS + amount + i] = EXT
    control[0] = amount

    apart = apart + [jnp.zeros((1, EXT), f32)]

    def row(k, i):
        return acc[i : i + 1, EXT * k : EXT * k + EXT]

    direct = [row(0, a) + row(0, 3 + a) for a in range(3)]
    total = [row(1, a) + row(1, 3 + a) for a in range(3)]
    gradient = []
    for a in range(3):
        for k in range(3):
            moment = row(1, 6 + 3 * k + a) + row(1, 15 + 3 * k + a)
            gradient.append(-3.0 * (apart[k] * total[a] - moment))
    zero = jnp.zeros((LANES - 12, 2 * LANES), f32)
    values = jnp.concatenate(direct + gradient + [zero], axis=0)
    out[...] = jnp.concatenate([values[:, :LANES].T, values[:, LANES:].T], axis=0)


def tile_of(own, ghosts, index, tile):
    if tile < BLOCKS // 8:
        return own[index, 8 * tile : 8 * tile + 8, :]
    d, n = divmod(tile - BLOCKS // 8, GHOST // 8)
    return ghosts[d][index, 8 * n : 8 * n + 8, :]


def near_force(control, own, ghosts, burg, parts, left, right, mask, acc, k_even, k_odd):
    shift = slot_shifts()
    one = jnp.ones((8, LANES), f32)
    low = lax.broadcasted_iota(jnp.int32, (8, LANES), 0) < 4

    for tile in range(EXT // 8):
        p = [tile_of(own, ghosts, k, tile) for k in range(3)]
        if tile >= BLOCKS // 8:
            k, by = shift[(tile - BLOCKS // 8) // (GHOST // 8)]
            p[k] = p[k] + by
        p = [halves(x) for x in p]
        for half in range(2):
            x = [v[half] for v in p]
            values = []
            for v in x:
                h, m, l = split3(v)
                values += [h, h, m, m, h, l]
            values += list(split3(x[0] * x[0] + x[1] * x[1] + x[2] * x[2]))
            values += [one, one, one]
            left[2 * tile + half] = pair_rows(values).T.astype(bf16)
    left[EXT // 4] = jnp.zeros((LANES, LANES), bf16)
    x = [own[k] for k in range(3)]
    for k in range(3):
        for i, part in enumerate(split3(-2.0 * x[k])):
            parts[3 * k + i] = part
    for i, part in enumerate(split3(x[0] * x[0] + x[1] * x[1] + x[2] * x[2] + core_sq)):
        parts[9 + i] = part
    for b in range(BLOCKS):
        def row(i):
            return jnp.broadcast_to(parts[i, b : b + 1, :], (8, LANES))

        rows = []
        for k in range(3):
            h, m, l = row(3 * k), row(3 * k + 1), row(3 * k + 2)
            high_mid = jnp.where(low, h, m)
            rows += [high_mid, high_mid, jnp.where(low, l, h)]
        rows += [one, jnp.where(low, one, row(9)), jnp.where(low, row(10), row(11))]
        for i in range(6):
            right[b, i] = jnp.concatenate(rows[2 * i : 2 * i + 2], axis=0).astype(bf16)
        right[b, 6:] = jnp.zeros((2, 16, LANES), bf16)
    place = lax.broadcasted_iota(jnp.int32, (16, LANES), 0) % 4
    for g in range(4):
        mask[g] = jnp.where(place == g, 1.0, 0.0).astype(bf16)

    acc[...] = jnp.zeros_like(acc)
    k_odd[...] = jnp.zeros_like(k_odd)

    def pair(i):
        word = control[AT_PAIRS + i]
        return lax.shift_right_logical(word, SHARE), word & (2**SHARE - 1)

    def half(step, k_now, k_before):
        for g in range(GROUP):
            if g % 2 == 0:
                i = (step - 1) * GROUP + g
                (b0, t0), (b1, t1) = pair(i), pair(i + 1)
                rows = jnp.concatenate(
                    [burg[pl.ds(pl.multiple_of(8 * t, 8), 8), :] for t in (t0, t1)], axis=0
                ).astype(bf16)
                both = jnp.dot(
                    jnp.concatenate([rows, rows], axis=1),
                    jnp.concatenate([k_before[g], k_before[g + 1]], axis=1),
                    preferred_element_type=f32,
                )
                at = pl.ds(pl.multiple_of(8 * b0, 8), 8)
                acc[at, :] = acc[at, :] + both[:8, :LANES]
                at = pl.ds(pl.multiple_of(8 * b1, 8), 8)
                acc[at, :] = acc[at, :] + both[8:, LANES:]
            b, t = pair(step * GROUP + g)
            features = (right[b] * mask[t & 3][None]).reshape(LANES, LANES)
            near_sq = jnp.dot(left[lax.shift_right_logical(t, 2)], features, preferred_element_type=f32)
            near_sq = jnp.maximum(near_sq, core_sq)
            r = lax.rsqrt(near_sq)
            q = lax.rsqrt(near_sq + (far_sq - core_sq))
            high, low = split2(r * r * r - q * q * q)
            k_now[g, :LANES, :] = high
            k_now[g, LANES:, :] = low

    def body(step, carry):
        half(2 * step, k_even, k_odd)
        half(2 * step + 1, k_odd, k_even)
        return carry

    steps = (control[0] + GROUP - 1) // GROUP + 1
    lax.fori_loop(0, (steps + 1) // 2, body, 0)


def component(acc, a):
    return acc[pl.ds(a, BLOCKS, stride=8), :] + acc[pl.ds(3 + a, BLOCKS, stride=8), :]


near_scratch = [
    pltpu.VMEM((12, BLOCKS, LANES), f32),
    pltpu.VMEM((EXT // 4 + 1, LANES, LANES), bf16),
    pltpu.VMEM((BLOCKS, 8, 16, LANES), bf16),
    pltpu.VMEM((4, 16, LANES), bf16),
    pltpu.VMEM((BLOCKS * 8, LANES), f32),
    pltpu.VMEM((GROUP, 2 * LANES, LANES), bf16),
    pltpu.VMEM((GROUP, 2 * LANES, LANES), bf16),
]


def total_force(expansion, near, places):
    out = []
    for a in range(3):
        far = expansion[0:1, a : a + 1]
        for k in range(3):
            far = far + expansion[0:1, 3 + 3 * a + k : 4 + 3 * a + k] * places[k]
        out.append(near[a] + far)
    return out


def first_kernel(
    control, shares, own, burgers, mobility, g3, g0, g2, g1,
    burg, expansion, moved, now, s0, s1, s2, s3, *scratch
):
    ghosts = (g0, g1, g2, g3)
    exists = slot_exists()
    burg[...] = jnp.zeros_like(burg)
    for tile in range(EXT // 8):
        for a in range(3):
            if tile < BLOCKS // 8:
                value = burgers[a, 8 * tile : 8 * tile + 8, :]
            else:
                d = (tile - BLOCKS // 8) // (GHOST // 8)
                value = tile_of(None, ghosts, 3 + a, tile)
                if exists[d] is not None:
                    value = jnp.where(exists[d], value, 0.0)
            high = round_bf16(value)
            burg[pl.ds(tile * 64 + a, 8, stride=8), :] = high
            burg[pl.ds(tile * 64 + 3 + a, 8, stride=8), :] = value - high
    expansion[...] = jnp.broadcast_to(jnp.sum(shares[...], axis=0, keepdims=True), (8, LANES))
    near_force(control, own, ghosts, burg, *scratch)
    acc = scratch[4]
    force = total_force(
        expansion[...], [component(acc, a) for a in range(3)], [own[k] for k in range(3)]
    )
    for a in range(3):
        step = (time_step * mobility[...]) * force[a]
        moved[a] = step
        now[a] = own[a] + step
    send_now(control, now, (s0, s1, s2, s3))


def step_kernel(
    final, control, expansion, own, g0, g1, g2, g3, burg, mobility, places, moved,
    new_moved, now, s0, s1, s2, s3, *scratch
):
    near_force(control, own, (g0, g1, g2, g3), burg, *scratch)
    acc = scratch[4]
    force = total_force(
        expansion[...], [component(acc, a) for a in range(3)], [own[k] for k in range(3)]
    )
    for a in range(3):
        total = moved[a] + (time_step * mobility[...]) * force[a]
        if final:
            put_rows(new_moved, a, total)
        else:
            new_moved[a] = total
        now[a] = places[a] + total
    send_now(control, now, (s0, s1, s2, s3))


def last_kernel(
    control, expansion, own, g0, g1, g2, g3, burg, mobility, velocity, *scratch
):
    near_force(control, own, (g0, g1, g2, g3), burg, *scratch)
    acc = scratch[4]
    force = total_force(
        expansion[...], [component(acc, a) for a in range(3)], [own[k] for k in range(3)]
    )
    for a in range(3):
        put_rows(velocity, a, mobility[...] * force[a])


def cost(flops):
    return pl.CostEstimate(flops=int(flops), bytes_accessed=2**20, transcendentals=0)


def shape(*dims, dtype=f32):
    return jax.ShapeDtypeStruct(dims, dtype)


def swap(x, slot):
    n_slabs, n_cells = lax.axis_size("slab"), lax.axis_size("cell")
    pairs = []
    for s in range(n_slabs):
        for c in range(n_cells):
            if slot == 0:
                to = (s ^ 1, c)
            elif slot == 3:
                to = (s, c ^ 1)
            elif slot == 1:
                t = s - 1 + 2 * (s % 2)
                to = (t, c) if 0 <= t < n_slabs else (s, c ^ 1)
            else:
                t = c - 1 + 2 * (c % 2)
                to = (s, t) if 0 <= t < n_cells else (s ^ 1, c)
            pairs.append((s * n_cells + c, to[0] * n_cells + to[1]))
    return lax.ppermute(x, ("slab", "cell"), pairs)


def exchange(sends):
    return [swap(x, slot) for slot, x in enumerate(sends)]


def local(positions, burgers, mobility, near_list, near_count, send_list):
    mobility = mobility.reshape(BLOCKS, LANES)
    flat = shape(*positions.shape)
    block = shape(3, BLOCKS, LANES)
    send = shape(3, GHOST, LANES)

    positions = positions.reshape(block.shape)
    burgers = burgers.reshape(block.shape)
    numbers = (
        jnp.pad(near_list.T, ((0, 16 - NEAR), (0, LANES - BLOCKS)))
        + jnp.pad(near_count[None], ((NEAR, 15 - NEAR), (0, LANES - BLOCKS)))
        + jnp.pad(send_list, ((8, 4), (0, LANES - GHOST)))
    )

    places, scalars, *sends = pl.pallas_call(
        pack_kernel,
        out_shape=[block, shape(16, LANES, dtype=jnp.int32)] + [shape(6, GHOST, LANES)] * 4,
        in_specs=[smem, vmem, vmem, vmem],
        out_specs=[vmem] * 6,
        compiler_params=params,
        name="pack",
    )(numbers, numbers, positions, burgers)
    ghosts = [swap(x, slot) for x, slot in zip(sends, (3, 0, 2, 1))]

    shares, control = pl.pallas_call(
        far_kernel,
        out_shape=[shape(EXT, LANES), shape(CONTROL, dtype=jnp.int32)],
        in_specs=[smem, vmem, vmem],
        out_specs=[vmem, smem],
        scratch_shapes=[
            pltpu.VMEM((32, 2 * EXT), f32),
            pltpu.VMEM((BLOCKS // 4, LANES, LANES), f32),
            pltpu.VMEM((BLOCKS // 4, LANES, LANES), bf16),
            pltpu.VMEM((4, LANES, EXT), bf16),
            pltpu.VMEM((4, 2 * LANES, 2 * EXT), bf16),
            pltpu.VMEM((4, 2 * LANES, 2 * EXT), bf16),
        ],
        compiler_params=params,
        cost_estimate=cost(20e9),
        name="far",
    )(scalars, places, burgers)
    shares = lax.all_to_all(shares, ("slab", "cell"), 0, 0, tiled=True)

    burg, expansion, moved, now, *sends = pl.pallas_call(
        first_kernel,
        out_shape=[shape((EXT + 1) * 8, LANES), shape(8, LANES), block, block] + [send] * 4,
        in_specs=[smem] + [vmem] * 8,
        out_specs=[vmem] * 8,
        scratch_shapes=near_scratch,
        compiler_params=params,
        cost_estimate=cost(20e9),
        name="near_first",
    )(control, shares, places, burgers, mobility, *ghosts)

    for substep in range(1, SUBSTEPS):
        final = substep == SUBSTEPS - 1
        ghosts = exchange(sends)
        moved, now, *sends = pl.pallas_call(
            functools.partial(step_kernel, final),
            out_shape=[flat if final else block, block] + [send] * 4,
            in_specs=[smem] + [vmem] * 10,
            out_specs=[vmem] * 6,
            scratch_shapes=near_scratch,
            compiler_params=params,
            cost_estimate=cost(20e9),
            name="near_step",
        )(control, expansion, now, *ghosts, burg, mobility, places, moved)

    ghosts = exchange(sends)
    velocity = pl.pallas_call(
        last_kernel,
        out_shape=flat,
        in_specs=[smem] + [vmem] * 8,
        out_specs=vmem,
        scratch_shapes=near_scratch,
        compiler_params=params,
        cost_estimate=cost(20e9),
        name="near_last",
    )(control, expansion, now, *ghosts, burg, mobility)
    return moved, velocity


def solution(mesh):
    return jax.shard_map(
        local,
        mesh=mesh,
        in_specs=(
            P(None, ("slab", "cell")),
            P(None, ("slab", "cell")),
            P(("slab", "cell")),
            P(("slab", "cell"), None),
            P(("slab", "cell")),
            P(None, ("slab", "cell")),
        ),
        out_specs=(P(None, ("slab", "cell")), P(None, ("slab", "cell"))),
        check_vma=False,
    )
```

profile of v0, /device:TPU:196, one launch (start us, length us, event | category | flops | bytes accessed | tf_op | source)
XLA Modules:
  0.0 133.9 jit_solution(3093660796764912003)
XLA Ops:
  0.6 1.0 copy_bitcast_fusion
  1.6 0.7 pad_add_fusion.numbers_smem.numbers
  2.3 1.5 %pack.1 = (f32[3,64,128]{2,1,0:T(8,128)S(1)}, s32[16,128]{1,0:T(8,128)S(1)}, f32[6,48,128]{2,1,0:T(8,128)S(1)}, f32[6,48,128]{2,1,0:T(8,128)S(1)}, f32[6,48,128]{2,1,0:T(8,128)S(1)}, /*index=5*/f32[6,48,128]{2,1,0:T(8,128)S(1)}) custom-call(s32[16,128]{1,0:T(8,128)S(1)} %pad_add_fusion.numbers_smem.numbers, s32[16,128]{1,0:T(8,128)S(1)} %pad_add_fusion.numbers_smem.numbers, ...), custom_call_target="tpu_custom_call" | custom-call | tf_op jit(solution)/shard_map/pack/pallas_call | solution.py:509
  3.9 7.3 %far.1 = (f32[256,128]{1,0:T(8,128)}, s32[656]{0:T(1024)S(1)}) custom-call(s32[16,128]{1,0:T(8,128)S(1)} %get-tuple-element.36.scalars, f32[3,64,128]{2,1,0:T(8,128)S(1)} %get-tuple-element.37.places.own, f32[3,64,128]{2,1,0:T(8,128)S(1)} %get-tuple-element.70.burgers), custom_call_target="tpu_custom_call" | custom-call | flops 20000000000 | bytes 1048576 | tf_op jit(solution)/shard_map/far/pallas_call | solution.py:519
  11.2 13.4 %all-to-all-start = ((f32[256,1,128]{2,1,0:T(1,128)}), f32[256,1,128]{2,1,0:T(1,128)S(1)}, u32[]{:S(2)}, u32[]{:S(2)}) async-start(f32[256,1,128]{2,1,0:T(1,128)} %bitcast.3), calls=%async_computation | async-start | bytes 262144 | tf_op jit(solution)/shard_map/all_to_all | solution.py:536
  24.9 1.5 %collective-permute-start.1 = (f32[6,48,128]{2,1,0:T(8,128)S(1)}, f32[6,48,128]{2,1,0:T(8,128)S(1)}, u32[]{:S(2)}, u32[]{:S(2)}) collective-permute-start(f32[6,48,128]{2,1,0:T(8,128)S(1)} %get-tuple-element.41), channel_id=1, source_target_pairs={{0,32},{1,33},{2,34},{3,35},{4,36},{5,37},{6,38},{7,39},{8,40},{9,... | collective-permute-start | bytes 442376 | tf_op jit(solution)/shard_map/ppermute | solution.py:488
  26.4 1.5 %collective-permute-start.2 = (f32[6,48,128]{2,1,0:T(8,128)S(1)}, f32[6,48,128]{2,1,0:T(8,128)S(1)}, u32[]{:S(2)}, u32[]{:S(2)}) collective-permute-start(f32[6,48,128]{2,1,0:T(8,128)S(1)} %get-tuple-element.42), channel_id=1, source_target_pairs={{0,32},{1,2},{2,1},{3,4},{4,3},{5,6},{6,5},{7,8},{8,7},{9,10},{10,... | collective-permute-start | bytes 442376 | tf_op jit(solution)/shard_map/ppermute | solution.py:488
  27.9 2.4 %collective-permute-start.3 = (f32[6,48,128]{2,1,0:T(8,128)S(1)}, f32[6,48,128]{2,1,0:T(8,128)S(1)}, u32[]{:S(2)}, u32[]{:S(2)}) collective-permute-start(f32[6,48,128]{2,1,0:T(8,128)S(1)} %get-tuple-element.43), channel_id=1, source_target_pairs={{0,1},{1,0},{2,3},{3,2},{4,5},{5,4},{6,7},{7,6},{8,9},{9,8},{10,11... | collective-permute-start | bytes 442376 | tf_op jit(solution)/shard_map/ppermute | solution.py:488
  30.3 1.1 collective-permute-done.1.g0
  32.0 5.3 %collective-permute-done.3.g1 = f32[6,48,128]{2,1,0:T(8,128)S(1)} collective-permute-done((f32[6,48,128]{2,1,0:T(8,128)S(1)}, f32[6,48,128]{2,1,0:T(8,128)S(1)}, u32[]{:S(2)}, u32[]{:S(2)}) %collective-permute-start.3) | collective-permute-done | bytes 147488 | tf_op jit(solution)/shard_map/ppermute | solution.py:488
  37.3 12.8 %near_first.1 = (f32[2056,128]{1,0:T(8,128)S(1)}, f32[8,128]{1,0:T(8,128)S(1)}, f32[3,64,128]{2,1,0:T(8,128)S(1)}, f32[3,64,128]{2,1,0:T(8,128)S(1)}, f32[3,48,1...) custom-call(s32[656]{0:T(1024)S(1)} %get-tuple-element.38.control, ...), custom_call_target="tpu_custom_call" | custom-call | flops 20000000000 | bytes 1048576 | tf_op jit(solution)/shard_map/near_first/pallas_call | solution.py:538
  50.4 0.9 collective-permute-start.7
  51.3 3.2 %collective-permute-done.4.g0 = f32[3,48,128]{2,1,0:T(8,128)S(1)} collective-permute-done((f32[3,48,128]{2,1,0:T(8,128)S(1)}, f32[3,48,128]{2,1,0:T(8,128)S(1)}, u32[]{:S(2)}, u32[]{:S(2)}) %collective-permute-start.4) | collective-permute-done | bytes 73760 | tf_op jit(solution)/shard_map/ppermute | solution.py:488
  54.5 3.7 %collective-permute-done.5.g1 = f32[3,48,128]{2,1,0:T(8,128)S(1)} collective-permute-done((f32[3,48,128]{2,1,0:T(8,128)S(1)}, f32[3,48,128]{2,1,0:T(8,128)S(1)}, u32[]{:S(2)}, u32[]{:S(2)}) %collective-permute-start.5) | collective-permute-done | bytes 73760 | tf_op jit(solution)/shard_map/ppermute | solution.py:488
  58.2 12.6 %near_step.3 = (f32[3,64,128]{2,1,0:T(8,128)S(1)}, f32[3,64,128]{2,1,0:T(8,128)S(1)}, f32[3,48,128]{2,1,0:T(8,128)S(1)}, f32[3,48,128]{2,1,0:T(8,128)S(1)}, f32[...) custom-call(s32[656]{0:T(1024)S(1)} %get-tuple-element.38.control, f32[8,128]{1,0:T(8,128)S(1)} %get-tuple-element.44.expansion, ...), custom_call_target="tpu_custom_call" | custom-call | flops 20000000000 | bytes 1048576 | tf_op jit(solution)/shard_map/near_step/pallas_call | solution.py:552
  71.4 3.9 %collective-permute-done.8.g0 = f32[3,48,128]{2,1,0:T(8,128)S(1)} collective-permute-done((f32[3,48,128]{2,1,0:T(8,128)S(1)}, f32[3,48,128]{2,1,0:T(8,128)S(1)}, u32[]{:S(2)}, u32[]{:S(2)}) %collective-permute-start.8) | collective-permute-done | bytes 73760 | tf_op jit(solution)/shard_map/ppermute | solution.py:488
  75.3 3.7 %collective-permute-done.9.g1 = f32[3,48,128]{2,1,0:T(8,128)S(1)} collective-permute-done((f32[3,48,128]{2,1,0:T(8,128)S(1)}, f32[3,48,128]{2,1,0:T(8,128)S(1)}, u32[]{:S(2)}, u32[]{:S(2)}) %collective-permute-start.9) | collective-permute-done | bytes 73760 | tf_op jit(solution)/shard_map/ppermute | solution.py:488
  79.0 12.6 %near_step.4 = (f32[3,64,128]{2,1,0:T(8,128)S(1)}, f32[3,64,128]{2,1,0:T(8,128)S(1)}, f32[3,48,128]{2,1,0:T(8,128)S(1)}, f32[3,48,128]{2,1,0:T(8,128)S(1)}, f32[...) custom-call(s32[656]{0:T(1024)S(1)} %get-tuple-element.38.control, f32[8,128]{1,0:T(8,128)S(1)} %get-tuple-element.44.expansion, ...), custom_call_target="tpu_custom_call" | custom-call | flops 20000000000 | bytes 1048576 | tf_op jit(solution)/shard_map/near_step/pallas_call | solution.py:552
  92.0 4.0 %collective-permute-done.12.g0 = f32[3,48,128]{2,1,0:T(8,128)S(1)} collective-permute-done((f32[3,48,128]{2,1,0:T(8,128)S(1)}, f32[3,48,128]{2,1,0:T(8,128)S(1)}, u32[]{:S(2)}, u32[]{:S(2)}) %collective-permute-start.12) | collective-permute-done | bytes 73760 | tf_op jit(solution)/shard_map/ppermute | solution.py:488
  96.0 3.7 %collective-permute-done.13.g1 = f32[3,48,128]{2,1,0:T(8,128)S(1)} collective-permute-done((f32[3,48,128]{2,1,0:T(8,128)S(1)}, f32[3,48,128]{2,1,0:T(8,128)S(1)}, u32[]{:S(2)}, u32[]{:S(2)}) %collective-permute-start.13) | collective-permute-done | bytes 73760 | tf_op jit(solution)/shard_map/ppermute | solution.py:488
  99.8 13.3 %near_step.5 = (f32[3,8192]{1,0:T(4,128)}, f32[3,64,128]{2,1,0:T(8,128)S(1)}, f32[3,48,128]{2,1,0:T(8,128)S(1)}, f32[3,48,128]{2,1,0:T(8,128)S(1)}, f32[3,48,128...) custom-call(s32[656]{0:T(1024)S(1)} %get-tuple-element.38.control, f32[8,128]{1,0:T(8,128)S(1)} %get-tuple-element.44.expansion, ...), custom_call_target="tpu_custom_call" | custom-call | flops 20000000000 | bytes 1048576 | tf_op jit(solution)/shard_map/near_step/pallas_call | solution.py:552
  113.2 4.2 %collective-permute-done.16.g0 = f32[3,48,128]{2,1,0:T(8,128)S(1)} collective-permute-done((f32[3,48,128]{2,1,0:T(8,128)S(1)}, f32[3,48,128]{2,1,0:T(8,128)S(1)}, u32[]{:S(2)}, u32[]{:S(2)}) %collective-permute-start.16) | collective-permute-done | bytes 73760 | tf_op jit(solution)/shard_map/ppermute | solution.py:488
  117.4 3.6 %collective-permute-done.17.g1 = f32[3,48,128]{2,1,0:T(8,128)S(1)} collective-permute-done((f32[3,48,128]{2,1,0:T(8,128)S(1)}, f32[3,48,128]{2,1,0:T(8,128)S(1)}, u32[]{:S(2)}, u32[]{:S(2)}) %collective-permute-start.17) | collective-permute-done | bytes 73760 | tf_op jit(solution)/shard_map/ppermute | solution.py:488
  121.0 12.9 %near_last.1 = f32[3,8192]{1,0:T(4,128)} custom-call(s32[656]{0:T(1024)S(1)} %get-tuple-element.38.control, f32[8,128]{1,0:T(8,128)S(1)} %get-tuple-element.44.expansion, f32[3,64,128]{2,1,0:T(8,128)S(1)} %get-tuple-element.65.own, f32[3,48,128]{2,1,0:T(8,128)S(1)} %collective-permute-done.16.g0, f32[3,48,128]{2,1,0:T(8,128)S(1)} %collective-permute-done.17.g1, ...), custom_call_target="tpu_custom_call" | custom-call | flops 20000000000 | bytes 1048576 | tf_op jit(solution)/shard_map/near_last/pallas_call | solution.py:564
  (29 shorter events, 2.2 us)
Async XLA Ops:
  3.8 33.5 %copy-start = (f32[8192]{0:T(1024)S(1)}, f32[8192]{0:T(1024)}, u32[]{:S(2)}) copy-start(f32[8192]{0:T(1024)} %param.8) | copy-start | bytes 98308
  11.2 26.1 %all-to-all-start = ((f32[256,1,128]{2,1,0:T(1,128)}), f32[256,1,128]{2,1,0:T(1,128)S(1)}, u32[]{:S(2)}, u32[]{:S(2)}) async-start(f32[256,1,128]{2,1,0:T(1,128)} %bitcast.3), calls=%async_computation | async-start | bytes 262144 | tf_op jit(solution)/shard_map/all_to_all | solution.py:536
  24.7 5.7 %collective-permute-start = (f32[6,48,128]{2,1,0:T(8,128)S(1)}, f32[6,48,128]{2,1,0:T(8,128)S(1)}, u32[]{:S(2)}, u32[]{:S(2)}) collective-permute-start(f32[6,48,128]{2,1,0:T(8,128)S(1)} %get-tuple-element.40), channel_id=1, source_target_pairs={{0,1},{1,0},{2,3},{3,2},{4,5},{5,4},{6,7},{7,6},{8,9},{9,8},{10,11... | collective-permute-start | bytes 442376 | tf_op jit(solution)/shard_map/ppermute | solution.py:488
  24.9 6.5 %collective-permute-start.1 = (f32[6,48,128]{2,1,0:T(8,128)S(1)}, f32[6,48,128]{2,1,0:T(8,128)S(1)}, u32[]{:S(2)}, u32[]{:S(2)}) collective-permute-start(f32[6,48,128]{2,1,0:T(8,128)S(1)} %get-tuple-element.41), channel_id=1, source_target_pairs={{0,32},{1,33},{2,34},{3,35},{4,36},{5,37},{6,38},{7,39},{8,40},{9,... | collective-permute-start | bytes 442376 | tf_op jit(solution)/shard_map/ppermute | solution.py:488
  26.4 5.6 %collective-permute-start.2 = (f32[6,48,128]{2,1,0:T(8,128)S(1)}, f32[6,48,128]{2,1,0:T(8,128)S(1)}, u32[]{:S(2)}, u32[]{:S(2)}) collective-permute-start(f32[6,48,128]{2,1,0:T(8,128)S(1)} %get-tuple-element.42), channel_id=1, source_target_pairs={{0,32},{1,2},{2,1},{3,4},{4,3},{5,6},{6,5},{7,8},{8,7},{9,10},{10,... | collective-permute-start | bytes 442376 | tf_op jit(solution)/shard_map/ppermute | solution.py:488
  27.9 9.4 %collective-permute-start.3 = (f32[6,48,128]{2,1,0:T(8,128)S(1)}, f32[6,48,128]{2,1,0:T(8,128)S(1)}, u32[]{:S(2)}, u32[]{:S(2)}) collective-permute-start(f32[6,48,128]{2,1,0:T(8,128)S(1)} %get-tuple-element.43), channel_id=1, source_target_pairs={{0,1},{1,0},{2,3},{3,2},{4,5},{5,4},{6,7},{7,6},{8,9},{9,8},{10,11... | collective-permute-start | bytes 442376 | tf_op jit(solution)/shard_map/ppermute | solution.py:488
  50.1 4.4 %collective-permute-start.4 = (f32[3,48,128]{2,1,0:T(8,128)S(1)}, f32[3,48,128]{2,1,0:T(8,128)S(1)}, u32[]{:S(2)}, u32[]{:S(2)}) collective-permute-start(f32[3,48,128]{2,1,0:T(8,128)S(1)} %get-tuple-element.46), channel_id=1, source_target_pairs={{0,32},{1,33},{2,34},{3,35},{4,36},{5,37},{6,38},{7,39},{8,40},{9,... | collective-permute-start | bytes 221192 | tf_op jit(solution)/shard_map/ppermute | solution.py:488
  50.2 8.1 %collective-permute-start.5 = (f32[3,48,128]{2,1,0:T(8,128)S(1)}, f32[3,48,128]{2,1,0:T(8,128)S(1)}, u32[]{:S(2)}, u32[]{:S(2)}) collective-permute-start(f32[3,48,128]{2,1,0:T(8,128)S(1)} %get-tuple-element.47), channel_id=1, source_target_pairs={{0,1},{1,0},{2,3},{3,2},{4,5},{5,4},{6,7},{7,6},{8,9},{9,8},{10,11... | collective-permute-start | bytes 221192 | tf_op jit(solution)/shard_map/ppermute | solution.py:488
  50.3 8.0 %collective-permute-start.6 = (f32[3,48,128]{2,1,0:T(8,128)S(1)}, f32[3,48,128]{2,1,0:T(8,128)S(1)}, u32[]{:S(2)}, u32[]{:S(2)}) collective-permute-start(f32[3,48,128]{2,1,0:T(8,128)S(1)} %get-tuple-element.48), channel_id=1, source_target_pairs={{0,32},{1,2},{2,1},{3,4},{4,3},{5,6},{6,5},{7,8},{8,7},{9,10},{10,... | collective-permute-start | bytes 221192 | tf_op jit(solution)/shard_map/ppermute | solution.py:488
  50.4 7.9 %collective-permute-start.7 = (f32[3,48,128]{2,1,0:T(8,128)S(1)}, f32[3,48,128]{2,1,0:T(8,128)S(1)}, u32[]{:S(2)}, u32[]{:S(2)}) collective-permute-start(f32[3,48,128]{2,1,0:T(8,128)S(1)} %get-tuple-element.49), channel_id=1, source_target_pairs={{0,1},{1,0},{2,3},{3,2},{4,5},{5,4},{6,7},{7,6},{8,9},{9,8},{10,11... | collective-permute-start | bytes 221192 | tf_op jit(solution)/shard_map/ppermute | solution.py:488
  70.8 4.4 %collective-permute-start.8 = (f32[3,48,128]{2,1,0:T(8,128)S(1)}, f32[3,48,128]{2,1,0:T(8,128)S(1)}, u32[]{:S(2)}, u32[]{:S(2)}) collective-permute-start(f32[3,48,128]{2,1,0:T(8,128)S(1)} %get-tuple-element.53), channel_id=1, source_target_pairs={{0,32},{1,33},{2,34},{3,35},{4,36},{5,37},{6,38},{7,39},{8,40},{9,... | collective-permute-start | bytes 221192 | tf_op jit(solution)/shard_map/ppermute | solution.py:488
  70.9 8.1 %collective-permute-start.9 = (f32[3,48,128]{2,1,0:T(8,128)S(1)}, f32[3,48,128]{2,1,0:T(8,128)S(1)}, u32[]{:S(2)}, u32[]{:S(2)}) collective-permute-start(f32[3,48,128]{2,1,0:T(8,128)S(1)} %get-tuple-element.54), channel_id=1, source_target_pairs={{0,1},{1,0},{2,3},{3,2},{4,5},{5,4},{6,7},{7,6},{8,9},{9,8},{10,11... | collective-permute-start | bytes 221192 | tf_op jit(solution)/shard_map/ppermute | solution.py:488
  71.0 8.0 %collective-permute-start.10 = (f32[3,48,128]{2,1,0:T(8,128)S(1)}, f32[3,48,128]{2,1,0:T(8,128)S(1)}, u32[]{:S(2)}, u32[]{:S(2)}) collective-permute-start(f32[3,48,128]{2,1,0:T(8,128)S(1)} %get-tuple-element.55), channel_id=1, source_target_pairs={{0,32},{1,2},{2,1},{3,4},{4,3},{5,6},{6,5},{7,8},{8,7},{9,10},{10,... | collective-permute-start | bytes 221192 | tf_op jit(solution)/shard_map/ppermute | solution.py:488
  71.3 7.7 %collective-permute-start.11 = (f32[3,48,128]{2,1,0:T(8,128)S(1)}, f32[3,48,128]{2,1,0:T(8,128)S(1)}, u32[]{:S(2)}, u32[]{:S(2)}) collective-permute-start(f32[3,48,128]{2,1,0:T(8,128)S(1)} %get-tuple-element.56), channel_id=1, source_target_pairs={{0,1},{1,0},{2,3},{3,2},{4,5},{5,4},{6,7},{7,6},{8,9},{9,8},{10,11... | collective-permute-start | bytes 221192 | tf_op jit(solution)/shard_map/ppermute | solution.py:488
  91.6 4.4 %collective-permute-start.12 = (f32[3,48,128]{2,1,0:T(8,128)S(1)}, f32[3,48,128]{2,1,0:T(8,128)S(1)}, u32[]{:S(2)}, u32[]{:S(2)}) collective-permute-start(f32[3,48,128]{2,1,0:T(8,128)S(1)} %get-tuple-element.59), channel_id=1, source_target_pairs={{0,32},{1,33},{2,34},{3,35},{4,36},{5,37},{6,38},{7,39},{8,40},{9,... | collective-permute-start | bytes 221192 | tf_op jit(solution)/shard_map/ppermute | solution.py:488
  91.7 8.1 %collective-permute-start.13 = (f32[3,48,128]{2,1,0:T(8,128)S(1)}, f32[3,48,128]{2,1,0:T(8,128)S(1)}, u32[]{:S(2)}, u32[]{:S(2)}) collective-permute-start(f32[3,48,128]{2,1,0:T(8,128)S(1)} %get-tuple-element.60), channel_id=1, source_target_pairs={{0,1},{1,0},{2,3},{3,2},{4,5},{5,4},{6,7},{7,6},{8,9},{9,8},{10,11... | collective-permute-start | bytes 221192 | tf_op jit(solution)/shard_map/ppermute | solution.py:488
  91.8 8.0 %collective-permute-start.14 = (f32[3,48,128]{2,1,0:T(8,128)S(1)}, f32[3,48,128]{2,1,0:T(8,128)S(1)}, u32[]{:S(2)}, u32[]{:S(2)}) collective-permute-start(f32[3,48,128]{2,1,0:T(8,128)S(1)} %get-tuple-element.61), channel_id=1, source_target_pairs={{0,32},{1,2},{2,1},{3,4},{4,3},{5,6},{6,5},{7,8},{8,7},{9,10},{10,... | collective-permute-start | bytes 221192 | tf_op jit(solution)/shard_map/ppermute | solution.py:488
  91.9 7.9 %collective-permute-start.15 = (f32[3,48,128]{2,1,0:T(8,128)S(1)}, f32[3,48,128]{2,1,0:T(8,128)S(1)}, u32[]{:S(2)}, u32[]{:S(2)}) collective-permute-start(f32[3,48,128]{2,1,0:T(8,128)S(1)} %get-tuple-element.62), channel_id=1, source_target_pairs={{0,1},{1,0},{2,3},{3,2},{4,5},{5,4},{6,7},{7,6},{8,9},{9,8},{10,11... | collective-permute-start | bytes 221192 | tf_op jit(solution)/shard_map/ppermute | solution.py:488
  113.0 4.4 %collective-permute-start.16 = (f32[3,48,128]{2,1,0:T(8,128)S(1)}, f32[3,48,128]{2,1,0:T(8,128)S(1)}, u32[]{:S(2)}, u32[]{:S(2)}) collective-permute-start(f32[3,48,128]{2,1,0:T(8,128)S(1)} %get-tuple-element.66), channel_id=1, source_target_pairs={{0,32},{1,33},{2,34},{3,35},{4,36},{5,37},{6,38},{7,39},{8,40},{9,... | collective-permute-start | bytes 221192 | tf_op jit(solution)/shard_map/ppermute | solution.py:488
  113.0 8.0 %collective-permute-start.17 = (f32[3,48,128]{2,1,0:T(8,128)S(1)}, f32[3,48,128]{2,1,0:T(8,128)S(1)}, u32[]{:S(2)}, u32[]{:S(2)}) collective-permute-start(f32[3,48,128]{2,1,0:T(8,128)S(1)} %get-tuple-element.67), channel_id=1, source_target_pairs={{0,1},{1,0},{2,3},{3,2},{4,5},{5,4},{6,7},{7,6},{8,9},{9,8},{10,11... | collective-permute-start | bytes 221192 | tf_op jit(solution)/shard_map/ppermute | solution.py:488
  113.0 8.0 %collective-permute-start.18 = (f32[3,48,128]{2,1,0:T(8,128)S(1)}, f32[3,48,128]{2,1,0:T(8,128)S(1)}, u32[]{:S(2)}, u32[]{:S(2)}) collective-permute-start(f32[3,48,128]{2,1,0:T(8,128)S(1)} %get-tuple-element.68), channel_id=1, source_target_pairs={{0,32},{1,2},{2,1},{3,4},{4,3},{5,6},{6,5},{7,8},{8,7},{9,10},{10,... | collective-permute-start | bytes 221192 | tf_op jit(solution)/shard_map/ppermute | solution.py:488
  113.1 8.0 %collective-permute-start.19 = (f32[3,48,128]{2,1,0:T(8,128)S(1)}, f32[3,48,128]{2,1,0:T(8,128)S(1)}, u32[]{:S(2)}, u32[]{:S(2)}) collective-permute-start(f32[3,48,128]{2,1,0:T(8,128)S(1)} %get-tuple-element.69), channel_id=1, source_target_pairs={{0,1},{1,0},{2,3},{3,2},{4,5},{5,4},{6,7},{7,6},{8,9},{9,8},{10,11... | collective-permute-start | bytes 221192 | tf_op jit(solution)/shard_map/ppermute | solution.py:488
where the time goes:
time: 134 us
  Pallas kernels  72.9 us (54%)
  waiting for transfers between devices  37.1 us (28%)
  starting transfers between devices  21.3 us (16%)
    pallas_call x3, Pallas kernels, local(): pl.pallas_call(functools.partial(step_kernel, final), out_shape=[flat if...  38.5 us
    ppermute x20, waiting for transfers between devices, swap(): return lax.ppermute(x, ('slab', 'cell'), pairs)  37.1 us
    all_to_all x1, starting transfers between devices, local(): shares = lax.all_to_all(shares, ('slab', 'cell'), 0, 0, tiled=True)  13.4 us
    pallas_call x1, Pallas kernels, local(): pl.pallas_call(last_kernel, out_shape=flat, in_specs=[smem] + [vmem] * 8,...  12.9 us
    pallas_call x1, Pallas kernels, local(): pl.pallas_call(first_kernel, out_shape=[shape((EXT + 1) * 8, LANES), shap...  12.8 us
    ppermute x20, starting transfers between devices, swap(): return lax.ppermute(x, ('slab', 'cell'), pairs)  7.9 us
    pallas_call x1, Pallas kernels, local(): pl.pallas_call(far_kernel, out_shape=[shape(EXT, LANES), shape(CONTROL, d...  7.34 us
  transfers between devices with their start and end apart: 21, of which 11 were waited for; matrix products, arithmetic and copies ran while one was open for 0% of the time, Pallas kernels for 0%

commit v1 on v0

--- a/solution.py
+++ b/solution.py
@@ -296,16 +296,22 @@
         if tile >= BLOCKS // 8:
             k, by = shift[(tile - BLOCKS // 8) // (GHOST // 8)]
             p[k] = p[k] + by
-        p = [halves(x) for x in p]
+        parts_of = [split3(x) for x in p]
+        parts_of.append(split3(p[0] * p[0] + p[1] * p[1] + p[2] * p[2]))
+        turned = [[pltpu.roll(x, 4, 0) for x in group] for group in parts_of]
         for half in range(2):
-            x = [v[half] for v in p]
+            first, second = (parts_of, turned) if half == 0 else (turned, parts_of)
             values = []
-            for v in x:
-                h, m, l = split3(v)
-                values += [h, h, m, m, h, l]
-            values += list(split3(x[0] * x[0] + x[1] * x[1] + x[2] * x[2]))
-            values += [one, one, one]
-            left[2 * tile + half] = pair_rows(values).T.astype(bf16)
+            for (h, m, _), (h2, m2, l2) in zip(first[:3], second[:3]):
+                values += [
+                    jnp.where(low, h, h2),
+                    jnp.where(low, m, m2),
+                    jnp.where(low, h, l2),
+                ]
+            h, _, l = first[3]
+            values += [jnp.where(low, h, second[3][1]), jnp.where(low, l, one), one]
+            values += [jnp.zeros((8, LANES), f32)] * (LANES // 8 - len(values))
+            left[2 * tile + half] = jnp.concatenate(values, axis=0).T.astype(bf16)
     left[EXT // 4] = jnp.zeros((LANES, LANES), bf16)
     x = [own[k] for k in range(3)]
     for k in range(3):
@@ -337,26 +343,31 @@
         word = control[AT_PAIRS + i]
         return lax.shift_right_logical(word, SHARE), word & (2**SHARE - 1)
 
+    def sums(step, g, k_before):
+        i = step * GROUP + g
+        (b0, t0), (b1, t1) = pair(i), pair(i + 1)
+        rows = jnp.concatenate(
+            [burg[pl.ds(pl.multiple_of(8 * t, 8), 8), :] for t in (t0, t1)], axis=0
+        ).astype(bf16)
+        both = jnp.dot(
+            jnp.concatenate([rows, rows], axis=1),
+            jnp.concatenate([k_before[g], k_before[g + 1]], axis=1),
+            preferred_element_type=f32,
+        )
+        at = pl.ds(pl.multiple_of(8 * b0, 8), 8)
+        acc[at, :] = acc[at, :] + both[:8, :LANES]
+        at = pl.ds(pl.multiple_of(8 * b1, 8), 8)
+        acc[at, :] = acc[at, :] + both[8:, LANES:]
+
     def half(step, k_now, k_before):
         for g in range(GROUP):
             if g % 2 == 0:
-                i = (step - 1) * GROUP + g
-                (b0, t0), (b1, t1) = pair(i), pair(i + 1)
-                rows = jnp.concatenate(
-                    [burg[pl.ds(pl.multiple_of(8 * t, 8), 8), :] for t in (t0, t1)], axis=0
-                ).astype(bf16)
-                both = jnp.dot(
-                    jnp.concatenate([rows, rows], axis=1),
-                    jnp.concatenate([k_before[g], k_before[g + 1]], axis=1),
-                    preferred_element_type=f32,
-                )
-                at = pl.ds(pl.multiple_of(8 * b0, 8), 8)
-                acc[at, :] = acc[at, :] + both[:8, :LANES]
-                at = pl.ds(pl.multiple_of(8 * b1, 8), 8)
-                acc[at, :] = acc[at, :] + both[8:, LANES:]
+                sums(step - 1, g, k_before)
             b, t = pair(step * GROUP + g)
             features = (right[b] * mask[t & 3][None]).reshape(LANES, LANES)
-            near_sq = jnp.dot(left[lax.shift_right_logical(t, 2)], features, preferred_element_type=f32)
+            near_sq = jnp.dot(
+                left[lax.shift_right_logical(t, 2)], features, preferred_element_type=f32
+            )
             near_sq = jnp.maximum(near_sq, core_sq)
             r = lax.rsqrt(near_sq)
             q = lax.rsqrt(near_sq + (far_sq - core_sq))
@@ -369,8 +380,10 @@
         half(2 * step + 1, k_odd, k_even)
         return carry
 
-    steps = (control[0] + GROUP - 1) // GROUP + 1
-    lax.fori_loop(0, (steps + 1) // 2, body, 0)
+    steps = (control[0] + 2 * GROUP - 1) // (2 * GROUP)
+    lax.fori_loop(0, steps, body, 0)
+    for g in range(0, GROUP, 2):
+        sums(2 * steps - 1, g, k_odd)
 
 
 def component(acc, a):
@@ -399,8 +412,7 @@
 
 
 def first_kernel(
-    control, shares, own, burgers, mobility, g3, g0, g2, g1,
-    burg, expansion, moved, now, s0, s1, s2, s3, *scratch
+    control, own, burgers, g3, g0, g2, g1, near, burg, *scratch
 ):
     ghosts = (g0, g1, g2, g3)
     exists = slot_exists()
@@ -417,17 +429,21 @@
             high = round_bf16(value)
             burg[pl.ds(tile * 64 + a, 8, stride=8), :] = high
             burg[pl.ds(tile * 64 + 3 + a, 8, stride=8), :] = value - high
-    expansion[...] = jnp.broadcast_to(jnp.sum(shares[...], axis=0, keepdims=True), (8, LANES))
     near_force(control, own, ghosts, burg, *scratch)
     acc = scratch[4]
-    force = total_force(
-        expansion[...], [component(acc, a) for a in range(3)], [own[k] for k in range(3)]
-    )
+    for a in range(3):
+        near[a] = component(acc, a)
+
+
+def start_kernel(control, shares, near, places, mobility, expansion, moved, now, *sends):
+    expansion[...] = jnp.broadcast_to(jnp.sum(shares[...], axis=0, keepdims=True), (8, LANES))
+    p = [places[k] for k in range(3)]
+    force = total_force(expansion[...], [near[a] for a in range(3)], p)
     for a in range(3):
         step = (time_step * mobility[...]) * force[a]
         moved[a] = step
-        now[a] = own[a] + step
-    send_now(control, now, (s0, s1, s2, s3))
+        now[a] = p[a] + step
+    send_now(control, now, sends)
 
 
 def step_kernel(
@@ -535,16 +551,25 @@
     )(scalars, places, burgers)
     shares = lax.all_to_all(shares, ("slab", "cell"), 0, 0, tiled=True)
 
-    burg, expansion, moved, now, *sends = pl.pallas_call(
+    near, burg = pl.pallas_call(
         first_kernel,
-        out_shape=[shape((EXT + 1) * 8, LANES), shape(8, LANES), block, block] + [send] * 4,
-        in_specs=[smem] + [vmem] * 8,
-        out_specs=[vmem] * 8,
+        out_shape=[block, shape((EXT + 1) * 8, LANES)],
+        in_specs=[smem] + [vmem] * 6,
+        out_specs=[vmem] * 2,
         scratch_shapes=near_scratch,
         compiler_params=params,
         cost_estimate=cost(20e9),
         name="near_first",
-    )(control, shares, places, burgers, mobility, *ghosts)
+    )(control, places, burgers, *ghosts)
+
+    expansion, moved, now, *sends = pl.pallas_call(
+        start_kernel,
+        out_shape=[shape(8, LANES), block, block] + [send] * 4,
+        in_specs=[smem] + [vmem] * 4,
+        out_specs=[vmem] * 7,
+        compiler_params=params,
+        name="start",
+    )(control, shares, near, places, mobility)
 
     for substep in range(1, SUBSTEPS):
         final = substep == SUBSTEPS - 1

time: 134 us -> 123 us (0.918)
  the two profiles are of different devices: /device:TPU:196 before, /device:TPU:102 now
where the time goes in v1:
time: 123 us; the launch traced here: 121 us
  Pallas kernels  68 us (55%)
  starting transfers between devices  27.6 us (22%)
  waiting for transfers between devices  23.2 us (19%)
    pallas_call x3, Pallas kernels, local(): pl.pallas_call(functools.partial(step_kernel, final), out_shape=[flat if...  35.1 us
    ppermute x20, waiting for transfers between devices, swap(): return lax.ppermute(x, ('slab', 'cell'), pairs)  23.2 us
    ppermute x20, starting transfers between devices, swap(): return lax.ppermute(x, ('slab', 'cell'), pairs)  15.9 us
    pallas_call x1, Pallas kernels, local(): pl.pallas_call(last_kernel, out_shape=flat, in_specs=[smem] + [vmem] * 8,...  11.8 us
    all_to_all x1, starting transfers between devices, local(): shares = lax.all_to_all(shares, ('slab', 'cell'), 0, 0, tiled=True)  11.7 us
    pallas_call x1, Pallas kernels, local(): pl.pallas_call(first_kernel, out_shape=[block, shape((EXT + 1) * 8, LANES...  11.2 us
    pallas_call x1, Pallas kernels, local(): pl.pallas_call(far_kernel, out_shape=[shape(EXT, LANES), shape(CONTROL, d...  7.33 us
  transfers between devices with their start and end apart: 21, of which 8 were waited for; matrix products, arithmetic and copies ran while one was open for 0% of the time, Pallas kernels for 15%

profile of v1, /device:TPU:102, one launch (start us, length us, event | category | flops | bytes accessed | tf_op | source)
XLA Modules:
  0.0 121.3 jit_solution(15938357699764196061)
XLA Ops:
  0.6 1.0 copy_bitcast_fusion
  2.3 1.5 %pack.1 = (f32[3,64,128]{2,1,0:T(8,128)S(1)}, s32[16,128]{1,0:T(8,128)S(1)}, f32[6,48,128]{2,1,0:T(8,128)S(1)}, f32[6,48,128]{2,1,0:T(8,128)S(1)}, f32[6,48,128]{2,1,0:T(8,128)S(1)}, /*index=5*/f32[6,48,128]{2,1,0:T(8,128)S(1)}) custom-call(s32[16,128]{1,0:T(8,128)S(1)} %pad_add_fusion.numbers_smem.numbers, s32[16,128]{1,0:T(8,128)S(1)} %pad_add_fusion.numbers_smem.numbers, ...), custom_call_target="tpu_custom_call" | custom-call | tf_op jit(solution)/shard_map/pack/pallas_call | solution.py:525
  3.9 1.7 %collective-permute-start.1 = (f32[6,48,128]{2,1,0:T(8,128)S(1)}, f32[6,48,128]{2,1,0:T(8,128)S(1)}, u32[]{:S(2)}, u32[]{:S(2)}) collective-permute-start(f32[6,48,128]{2,1,0:T(8,128)S(1)} %get-tuple-element.42), channel_id=1, source_target_pairs={{0,32},{1,33},{2,34},{3,35},{4,36},{5,37},{6,38},{7,39},{8,40},{9,... | collective-permute-start | bytes 442376 | tf_op jit(solution)/shard_map/ppermute | solution.py:504
  6.2 2.7 %collective-permute-start.3 = (f32[6,48,128]{2,1,0:T(8,128)S(1)}, f32[6,48,128]{2,1,0:T(8,128)S(1)}, u32[]{:S(2)}, u32[]{:S(2)}) collective-permute-start(f32[6,48,128]{2,1,0:T(8,128)S(1)} %get-tuple-element.44), channel_id=1, source_target_pairs={{0,1},{1,0},{2,3},{3,2},{4,5},{5,4},{6,7},{7,6},{8,9},{9,8},{10,11... | collective-permute-start | bytes 442376 | tf_op jit(solution)/shard_map/ppermute | solution.py:504
  8.9 7.3 %far.1 = (f32[256,128]{1,0:T(8,128)}, s32[656]{0:T(1024)S(1)}) custom-call(s32[16,128]{1,0:T(8,128)S(1)} %get-tuple-element.37.scalars, f32[3,64,128]{2,1,0:T(8,128)S(1)} %get-tuple-element.38.places.own, f32[3,64,128]{2,1,0:T(8,128)S(1)} %get-tuple-element.72.burgers), custom_call_target="tpu_custom_call" | custom-call | flops 20000000000 | bytes 1048576 | tf_op jit(solution)/shard_map/far/pallas_call | solution.py:535
  16.3 11.7 %all-to-all-start = ((f32[256,1,128]{2,1,0:T(1,128)}), f32[256,1,128]{2,1,0:T(1,128)S(1)}, u32[]{:S(2)}, u32[]{:S(2)}) async-start(f32[256,1,128]{2,1,0:T(1,128)} %bitcast.3), calls=%async_computation | async-start | bytes 262144 | tf_op jit(solution)/shard_map/all_to_all | solution.py:552
  28.0 11.2 %near_first.1 = (f32[3,64,128]{2,1,0:T(8,128)S(1)}, f32[2056,128]{1,0:T(8,128)S(1)}) custom-call(s32[656]{0:T(1024)S(1)} %get-tuple-element.39.control, f32[3,64,128]{2,1,0:T(8,128)S(1)} %get-tuple-element.38.places.own, f32[3,64,128]{2,1,0:T(8,128)S(1)} %get-tuple-element.72.burgers, f32[6,48,128]{2,1,0:T(8,128)S(1)} %collective-permute-done.g3, ...), custom_call_target="tpu_custom_call" | custom-call | flops 20000000000 | bytes 1048576 | tf_op jit(solution)/shard_map/near_first/pallas_call | solution.py:554
  39.2 1.1 start.1
  40.4 1.6 %collective-permute-start.4 = (f32[3,48,128]{2,1,0:T(8,128)S(1)}, f32[3,48,128]{2,1,0:T(8,128)S(1)}, u32[]{:S(2)}, u32[]{:S(2)}) collective-permute-start(f32[3,48,128]{2,1,0:T(8,128)S(1)} %get-tuple-element.48), channel_id=1, source_target_pairs={{0,32},{1,33},{2,34},{3,35},{4,36},{5,37},{6,38},{7,39},{8,40},{9,... | collective-permute-start | bytes 221192 | tf_op jit(solution)/shard_map/ppermute | solution.py:504
  42.0 2.4 %collective-permute-start.5 = (f32[3,48,128]{2,1,0:T(8,128)S(1)}, f32[3,48,128]{2,1,0:T(8,128)S(1)}, u32[]{:S(2)}, u32[]{:S(2)}) collective-permute-start(f32[3,48,128]{2,1,0:T(8,128)S(1)} %get-tuple-element.49), channel_id=1, source_target_pairs={{0,1},{1,0},{2,3},{3,2},{4,5},{5,4},{6,7},{7,6},{8,9},{9,8},{10,11... | collective-permute-start | bytes 221192 | tf_op jit(solution)/shard_map/ppermute | solution.py:504
  44.8 5.1 %collective-permute-done.5.g1 = f32[3,48,128]{2,1,0:T(8,128)S(1)} collective-permute-done((f32[3,48,128]{2,1,0:T(8,128)S(1)}, f32[3,48,128]{2,1,0:T(8,128)S(1)}, u32[]{:S(2)}, u32[]{:S(2)}) %collective-permute-start.5) | collective-permute-done | bytes 73760 | tf_op jit(solution)/shard_map/ppermute | solution.py:504
  49.9 11.5 %near_step.3 = (f32[3,64,128]{2,1,0:T(8,128)S(1)}, f32[3,64,128]{2,1,0:T(8,128)S(1)}, f32[3,48,128]{2,1,0:T(8,128)S(1)}, f32[3,48,128]{2,1,0:T(8,128)S(1)}, f32[...) custom-call(s32[656]{0:T(1024)S(1)} %get-tuple-element.39.control, f32[8,128]{1,0:T(8,128)S(1)} %get-tuple-element.46.expansion, ...), custom_call_target="tpu_custom_call" | custom-call | flops 20000000000 | bytes 1048576 | tf_op jit(solution)/shard_map/near_step/pallas_call | solution.py:577
  61.8 1.9 %collective-permute-start.10 = (f32[3,48,128]{2,1,0:T(8,128)S(1)}, f32[3,48,128]{2,1,0:T(8,128)S(1)}, u32[]{:S(2)}, u32[]{:S(2)}) collective-permute-start(f32[3,48,128]{2,1,0:T(8,128)S(1)} %get-tuple-element.57), channel_id=1, source_target_pairs={{0,32},{1,2},{2,1},{3,4},{4,3},{5,6},{6,5},{7,8},{8,7},{9,10},{10,... | collective-permute-start | bytes 221192 | tf_op jit(solution)/shard_map/ppermute | solution.py:504
  63.7 2.1 %collective-permute-done.8.g0 = f32[3,48,128]{2,1,0:T(8,128)S(1)} collective-permute-done((f32[3,48,128]{2,1,0:T(8,128)S(1)}, f32[3,48,128]{2,1,0:T(8,128)S(1)}, u32[]{:S(2)}, u32[]{:S(2)}) %collective-permute-start.8) | collective-permute-done | bytes 73760 | tf_op jit(solution)/shard_map/ppermute | solution.py:504
  65.8 3.9 %collective-permute-done.9.g1 = f32[3,48,128]{2,1,0:T(8,128)S(1)} collective-permute-done((f32[3,48,128]{2,1,0:T(8,128)S(1)}, f32[3,48,128]{2,1,0:T(8,128)S(1)}, u32[]{:S(2)}, u32[]{:S(2)}) %collective-permute-start.9) | collective-permute-done | bytes 73760 | tf_op jit(solution)/shard_map/ppermute | solution.py:504
  69.7 11.5 %near_step.4 = (f32[3,64,128]{2,1,0:T(8,128)S(1)}, f32[3,64,128]{2,1,0:T(8,128)S(1)}, f32[3,48,128]{2,1,0:T(8,128)S(1)}, f32[3,48,128]{2,1,0:T(8,128)S(1)}, f32[...) custom-call(s32[656]{0:T(1024)S(1)} %get-tuple-element.39.control, f32[8,128]{1,0:T(8,128)S(1)} %get-tuple-element.46.expansion, ...), custom_call_target="tpu_custom_call" | custom-call | flops 20000000000 | bytes 1048576 | tf_op jit(solution)/shard_map/near_step/pallas_call | solution.py:577
  81.4 1.9 %collective-permute-start.14 = (f32[3,48,128]{2,1,0:T(8,128)S(1)}, f32[3,48,128]{2,1,0:T(8,128)S(1)}, u32[]{:S(2)}, u32[]{:S(2)}) collective-permute-start(f32[3,48,128]{2,1,0:T(8,128)S(1)} %get-tuple-element.63), channel_id=1, source_target_pairs={{0,32},{1,2},{2,1},{3,4},{4,3},{5,6},{6,5},{7,8},{8,7},{9,10},{10,... | collective-permute-start | bytes 221192 | tf_op jit(solution)/shard_map/ppermute | solution.py:504
  83.4 2.3 %collective-permute-done.12.g0 = f32[3,48,128]{2,1,0:T(8,128)S(1)} collective-permute-done((f32[3,48,128]{2,1,0:T(8,128)S(1)}, f32[3,48,128]{2,1,0:T(8,128)S(1)}, u32[]{:S(2)}, u32[]{:S(2)}) %collective-permute-start.12) | collective-permute-done | bytes 73760 | tf_op jit(solution)/shard_map/ppermute | solution.py:504
  85.6 3.7 %collective-permute-done.13.g1 = f32[3,48,128]{2,1,0:T(8,128)S(1)} collective-permute-done((f32[3,48,128]{2,1,0:T(8,128)S(1)}, f32[3,48,128]{2,1,0:T(8,128)S(1)}, u32[]{:S(2)}, u32[]{:S(2)}) %collective-permute-start.13) | collective-permute-done | bytes 73760 | tf_op jit(solution)/shard_map/ppermute | solution.py:504
  89.4 12.2 %near_step.5 = (f32[3,8192]{1,0:T(4,128)}, f32[3,64,128]{2,1,0:T(8,128)S(1)}, f32[3,48,128]{2,1,0:T(8,128)S(1)}, f32[3,48,128]{2,1,0:T(8,128)S(1)}, f32[3,48,128...) custom-call(s32[656]{0:T(1024)S(1)} %get-tuple-element.39.control, f32[8,128]{1,0:T(8,128)S(1)} %get-tuple-element.46.expansion, ...), custom_call_target="tpu_custom_call" | custom-call | flops 20000000000 | bytes 1048576 | tf_op jit(solution)/shard_map/near_step/pallas_call | solution.py:577
  101.5 2.2 %collective-permute-start.18 = (f32[3,48,128]{2,1,0:T(8,128)S(1)}, f32[3,48,128]{2,1,0:T(8,128)S(1)}, u32[]{:S(2)}, u32[]{:S(2)}) collective-permute-start(f32[3,48,128]{2,1,0:T(8,128)S(1)} %get-tuple-element.70), channel_id=1, source_target_pairs={{0,32},{1,2},{2,1},{3,4},{4,3},{5,6},{6,5},{7,8},{8,7},{9,10},{10,... | collective-permute-start | bytes 221192 | tf_op jit(solution)/shard_map/ppermute | solution.py:504
  103.7 2.1 %collective-permute-done.16.g0 = f32[3,48,128]{2,1,0:T(8,128)S(1)} collective-permute-done((f32[3,48,128]{2,1,0:T(8,128)S(1)}, f32[3,48,128]{2,1,0:T(8,128)S(1)}, u32[]{:S(2)}, u32[]{:S(2)}) %collective-permute-start.16) | collective-permute-done | bytes 73760 | tf_op jit(solution)/shard_map/ppermute | solution.py:504
  105.9 3.6 %collective-permute-done.17.g1 = f32[3,48,128]{2,1,0:T(8,128)S(1)} collective-permute-done((f32[3,48,128]{2,1,0:T(8,128)S(1)}, f32[3,48,128]{2,1,0:T(8,128)S(1)}, u32[]{:S(2)}, u32[]{:S(2)}) %collective-permute-start.17) | collective-permute-done | bytes 73760 | tf_op jit(solution)/shard_map/ppermute | solution.py:504
  109.5 11.8 %near_last.1 = f32[3,8192]{1,0:T(4,128)} custom-call(s32[656]{0:T(1024)S(1)} %get-tuple-element.39.control, f32[8,128]{1,0:T(8,128)S(1)} %get-tuple-element.46.expansion, f32[3,64,128]{2,1,0:T(8,128)S(1)} %get-tuple-element.67.own, f32[3,48,128]{2,1,0:T(8,128)S(1)} %collective-permute-done.16.g0, f32[3,48,128]{2,1,0:T(8,128)S(1)} %collective-permute-done.17.g1, ...), custom_call_target="tpu_custom_call" | custom-call | flops 20000000000 | bytes 1048576 | tf_op jit(solution)/shard_map/near_last/pallas_call | solution.py:589
  (30 shorter events, 2.4 us)
Async XLA Ops:
  3.8 24.1 %collective-permute-start = (f32[6,48,128]{2,1,0:T(8,128)S(1)}, f32[6,48,128]{2,1,0:T(8,128)S(1)}, u32[]{:S(2)}, u32[]{:S(2)}) collective-permute-start(f32[6,48,128]{2,1,0:T(8,128)S(1)} %get-tuple-element.41), channel_id=1, source_target_pairs={{0,1},{1,0},{2,3},{3,2},{4,5},{5,4},{6,7},{7,6},{8,9},{9,8},{10,11... | collective-permute-start | bytes 442376 | tf_op jit(solution)/shard_map/ppermute | solution.py:504
  3.9 24.0 %collective-permute-start.1 = (f32[6,48,128]{2,1,0:T(8,128)S(1)}, f32[6,48,128]{2,1,0:T(8,128)S(1)}, u32[]{:S(2)}, u32[]{:S(2)}) collective-permute-start(f32[6,48,128]{2,1,0:T(8,128)S(1)} %get-tuple-element.42), channel_id=1, source_target_pairs={{0,32},{1,33},{2,34},{3,35},{4,36},{5,37},{6,38},{7,39},{8,40},{9,... | collective-permute-start | bytes 442376 | tf_op jit(solution)/shard_map/ppermute | solution.py:504
  5.6 22.3 %collective-permute-start.2 = (f32[6,48,128]{2,1,0:T(8,128)S(1)}, f32[6,48,128]{2,1,0:T(8,128)S(1)}, u32[]{:S(2)}, u32[]{:S(2)}) collective-permute-start(f32[6,48,128]{2,1,0:T(8,128)S(1)} %get-tuple-element.43), channel_id=1, source_target_pairs={{0,32},{1,2},{2,1},{3,4},{4,3},{5,6},{6,5},{7,8},{8,7},{9,10},{10,... | collective-permute-start | bytes 442376 | tf_op jit(solution)/shard_map/ppermute | solution.py:504
  6.2 21.8 %collective-permute-start.3 = (f32[6,48,128]{2,1,0:T(8,128)S(1)}, f32[6,48,128]{2,1,0:T(8,128)S(1)}, u32[]{:S(2)}, u32[]{:S(2)}) collective-permute-start(f32[6,48,128]{2,1,0:T(8,128)S(1)} %get-tuple-element.44), channel_id=1, source_target_pairs={{0,1},{1,0},{2,3},{3,2},{4,5},{5,4},{6,7},{7,6},{8,9},{9,8},{10,11... | collective-permute-start | bytes 442376 | tf_op jit(solution)/shard_map/ppermute | solution.py:504
  16.3 22.9 %all-to-all-start = ((f32[256,1,128]{2,1,0:T(1,128)}), f32[256,1,128]{2,1,0:T(1,128)S(1)}, u32[]{:S(2)}, u32[]{:S(2)}) async-start(f32[256,1,128]{2,1,0:T(1,128)} %bitcast.3), calls=%async_computation | async-start | bytes 262144 | tf_op jit(solution)/shard_map/all_to_all | solution.py:552
  28.0 11.2 %copy-start = (f32[8192]{0:T(1024)S(1)}, f32[8192]{0:T(1024)}, u32[]{:S(2)}) copy-start(f32[8192]{0:T(1024)} %param.8) | copy-start | bytes 98308
  40.4 4.4 %collective-permute-start.4 = (f32[3,48,128]{2,1,0:T(8,128)S(1)}, f32[3,48,128]{2,1,0:T(8,128)S(1)}, u32[]{:S(2)}, u32[]{:S(2)}) collective-permute-start(f32[3,48,128]{2,1,0:T(8,128)S(1)} %get-tuple-element.48), channel_id=1, source_target_pairs={{0,32},{1,33},{2,34},{3,35},{4,36},{5,37},{6,38},{7,39},{8,40},{9,... | collective-permute-start | bytes 221192 | tf_op jit(solution)/shard_map/ppermute | solution.py:504
  42.0 8.0 %collective-permute-start.5 = (f32[3,48,128]{2,1,0:T(8,128)S(1)}, f32[3,48,128]{2,1,0:T(8,128)S(1)}, u32[]{:S(2)}, u32[]{:S(2)}) collective-permute-start(f32[3,48,128]{2,1,0:T(8,128)S(1)} %get-tuple-element.49), channel_id=1, source_target_pairs={{0,1},{1,0},{2,3},{3,2},{4,5},{5,4},{6,7},{7,6},{8,9},{9,8},{10,11... | collective-permute-start | bytes 221192 | tf_op jit(solution)/shard_map/ppermute | solution.py:504
  44.3 5.6 %collective-permute-start.6 = (f32[3,48,128]{2,1,0:T(8,128)S(1)}, f32[3,48,128]{2,1,0:T(8,128)S(1)}, u32[]{:S(2)}, u32[]{:S(2)}) collective-permute-start(f32[3,48,128]{2,1,0:T(8,128)S(1)} %get-tuple-element.50), channel_id=1, source_target_pairs={{0,32},{1,2},{2,1},{3,4},{4,3},{5,6},{6,5},{7,8},{8,7},{9,10},{10,... | collective-permute-start | bytes 221192 | tf_op jit(solution)/shard_map/ppermute | solution.py:504
  44.4 5.6 %collective-permute-start.7 = (f32[3,48,128]{2,1,0:T(8,128)S(1)}, f32[3,48,128]{2,1,0:T(8,128)S(1)}, u32[]{:S(2)}, u32[]{:S(2)}) collective-permute-start(f32[3,48,128]{2,1,0:T(8,128)S(1)} %get-tuple-element.51), channel_id=1, source_target_pairs={{0,1},{1,0},{2,3},{3,2},{4,5},{5,4},{6,7},{7,6},{8,9},{9,8},{10,11... | collective-permute-start | bytes 221192 | tf_op jit(solution)/shard_map/ppermute | solution.py:504
  61.4 4.4 %collective-permute-start.8 = (f32[3,48,128]{2,1,0:T(8,128)S(1)}, f32[3,48,128]{2,1,0:T(8,128)S(1)}, u32[]{:S(2)}, u32[]{:S(2)}) collective-permute-start(f32[3,48,128]{2,1,0:T(8,128)S(1)} %get-tuple-element.55), channel_id=1, source_target_pairs={{0,32},{1,33},{2,34},{3,35},{4,36},{5,37},{6,38},{7,39},{8,40},{9,... | collective-permute-start | bytes 221192 | tf_op jit(solution)/shard_map/ppermute | solution.py:504
  61.5 8.2 %collective-permute-start.9 = (f32[3,48,128]{2,1,0:T(8,128)S(1)}, f32[3,48,128]{2,1,0:T(8,128)S(1)}, u32[]{:S(2)}, u32[]{:S(2)}) collective-permute-start(f32[3,48,128]{2,1,0:T(8,128)S(1)} %get-tuple-element.56), channel_id=1, source_target_pairs={{0,1},{1,0},{2,3},{3,2},{4,5},{5,4},{6,7},{7,6},{8,9},{9,8},{10,11... | collective-permute-start | bytes 221192 | tf_op jit(solution)/shard_map/ppermute | solution.py:504
  61.8 8.0 %collective-permute-start.10 = (f32[3,48,128]{2,1,0:T(8,128)S(1)}, f32[3,48,128]{2,1,0:T(8,128)S(1)}, u32[]{:S(2)}, u32[]{:S(2)}) collective-permute-start(f32[3,48,128]{2,1,0:T(8,128)S(1)} %get-tuple-element.57), channel_id=1, source_target_pairs={{0,32},{1,2},{2,1},{3,4},{4,3},{5,6},{6,5},{7,8},{8,7},{9,10},{10,... | collective-permute-start | bytes 221192 | tf_op jit(solution)/shard_map/ppermute | solution.py:504
  63.7 6.0 %collective-permute-start.11 = (f32[3,48,128]{2,1,0:T(8,128)S(1)}, f32[3,48,128]{2,1,0:T(8,128)S(1)}, u32[]{:S(2)}, u32[]{:S(2)}) collective-permute-start(f32[3,48,128]{2,1,0:T(8,128)S(1)} %get-tuple-element.58), channel_id=1, source_target_pairs={{0,1},{1,0},{2,3},{3,2},{4,5},{5,4},{6,7},{7,6},{8,9},{9,8},{10,11... | collective-permute-start | bytes 221192 | tf_op jit(solution)/shard_map/ppermute | solution.py:504
  81.2 4.4 %collective-permute-start.12 = (f32[3,48,128]{2,1,0:T(8,128)S(1)}, f32[3,48,128]{2,1,0:T(8,128)S(1)}, u32[]{:S(2)}, u32[]{:S(2)}) collective-permute-start(f32[3,48,128]{2,1,0:T(8,128)S(1)} %get-tuple-element.61), channel_id=1, source_target_pairs={{0,32},{1,33},{2,34},{3,35},{4,36},{5,37},{6,38},{7,39},{8,40},{9,... | collective-permute-start | bytes 221192 | tf_op jit(solution)/shard_map/ppermute | solution.py:504
  81.3 8.1 %collective-permute-start.13 = (f32[3,48,128]{2,1,0:T(8,128)S(1)}, f32[3,48,128]{2,1,0:T(8,128)S(1)}, u32[]{:S(2)}, u32[]{:S(2)}) collective-permute-start(f32[3,48,128]{2,1,0:T(8,128)S(1)} %get-tuple-element.62), channel_id=1, source_target_pairs={{0,1},{1,0},{2,3},{3,2},{4,5},{5,4},{6,7},{7,6},{8,9},{9,8},{10,11... | collective-permute-start | bytes 221192 | tf_op jit(solution)/shard_map/ppermute | solution.py:504
  81.4 8.0 %collective-permute-start.14 = (f32[3,48,128]{2,1,0:T(8,128)S(1)}, f32[3,48,128]{2,1,0:T(8,128)S(1)}, u32[]{:S(2)}, u32[]{:S(2)}) collective-permute-start(f32[3,48,128]{2,1,0:T(8,128)S(1)} %get-tuple-element.63), channel_id=1, source_target_pairs={{0,32},{1,2},{2,1},{3,4},{4,3},{5,6},{6,5},{7,8},{8,7},{9,10},{10,... | collective-permute-start | bytes 221192 | tf_op jit(solution)/shard_map/ppermute | solution.py:504
  83.4 6.0 %collective-permute-start.15 = (f32[3,48,128]{2,1,0:T(8,128)S(1)}, f32[3,48,128]{2,1,0:T(8,128)S(1)}, u32[]{:S(2)}, u32[]{:S(2)}) collective-permute-start(f32[3,48,128]{2,1,0:T(8,128)S(1)} %get-tuple-element.64), channel_id=1, source_target_pairs={{0,1},{1,0},{2,3},{3,2},{4,5},{5,4},{6,7},{7,6},{8,9},{9,8},{10,11... | collective-permute-start | bytes 221192 | tf_op jit(solution)/shard_map/ppermute | solution.py:504
  101.5 4.4 %collective-permute-start.16 = (f32[3,48,128]{2,1,0:T(8,128)S(1)}, f32[3,48,128]{2,1,0:T(8,128)S(1)}, u32[]{:S(2)}, u32[]{:S(2)}) collective-permute-start(f32[3,48,128]{2,1,0:T(8,128)S(1)} %get-tuple-element.68), channel_id=1, source_target_pairs={{0,32},{1,33},{2,34},{3,35},{4,36},{5,37},{6,38},{7,39},{8,40},{9,... | collective-permute-start | bytes 221192 | tf_op jit(solution)/shard_map/ppermute | solution.py:504
  101.5 8.0 %collective-permute-start.17 = (f32[3,48,128]{2,1,0:T(8,128)S(1)}, f32[3,48,128]{2,1,0:T(8,128)S(1)}, u32[]{:S(2)}, u32[]{:S(2)}) collective-permute-start(f32[3,48,128]{2,1,0:T(8,128)S(1)} %get-tuple-element.69), channel_id=1, source_target_pairs={{0,1},{1,0},{2,3},{3,2},{4,5},{5,4},{6,7},{7,6},{8,9},{9,8},{10,11... | collective-permute-start | bytes 221192 | tf_op jit(solution)/shard_map/ppermute | solution.py:504
  101.5 8.0 %collective-permute-start.18 = (f32[3,48,128]{2,1,0:T(8,128)S(1)}, f32[3,48,128]{2,1,0:T(8,128)S(1)}, u32[]{:S(2)}, u32[]{:S(2)}) collective-permute-start(f32[3,48,128]{2,1,0:T(8,128)S(1)} %get-tuple-element.70), channel_id=1, source_target_pairs={{0,32},{1,2},{2,1},{3,4},{4,3},{5,6},{6,5},{7,8},{8,7},{9,10},{10,... | collective-permute-start | bytes 221192 | tf_op jit(solution)/shard_map/ppermute | solution.py:504
  103.7 5.8 %collective-permute-start.19 = (f32[3,48,128]{2,1,0:T(8,128)S(1)}, f32[3,48,128]{2,1,0:T(8,128)S(1)}, u32[]{:S(2)}, u32[]{:S(2)}) collective-permute-start(f32[3,48,128]{2,1,0:T(8,128)S(1)} %get-tuple-element.71), channel_id=1, source_target_pairs={{0,1},{1,0},{2,3},{3,2},{4,5},{5,4},{6,7},{7,6},{8,9},{9,8},{10,11... | collective-permute-start | bytes 221192 | tf_op jit(solution)/shard_map/ppermute | solution.py:504
